TPU v7x, 256 devices: a whole 4x4x8 slice. The times are simulated.
256 devices in a mesh: depth: 16 (over x, y), img: 16 (over z, core).
Axes of the slice: x: 4, y: 4, z: 8, core: 2. Of those that a mesh axis runs over, the one named last changes fastest.
Arguments:
- velocity: float32 [3, 128, 16, 256, 256], P(None, 'depth', 'img'), may hold values from -6 to 6
- emission: float32 [3, 8], replicated, may hold values from 0 to 2
- extinction: float32 [8], replicated, may hold values from 0.4 to 4
Outputs:
- picture: float32 [4, 16, 256, 256], P(None, 'img')
All inputs are finite; a program needn't handle non-finite values.
Results may differ from a plain program's by a relative error of at most 0.0003.
Values sent between devices are 32-bit elements; how exact they have to be, the bound alone decides.
A program may use at most 128 MiB of HBM per device.

v0:
```python
import functools

import jax
import jax.numpy as jnp
from jax import lax
from jax.experimental import pallas as pl
from jax.experimental.pallas import tpu as pltpu
from jax.sharding import PartitionSpec as P

F32 = jnp.float32
LANES = 128
SUB = 8
CHUNKS = 2
TINY = 1.2e-38


def kernel(
    vel, emi, ext, out,
    uxy, uz, st, pack_l, pack_r, rim_l, rim_r, spack_l, spack_r, srim_l, srim_r,
    part, parts, done,
    loc_sem, face_send, face_recv, rim_send, rim_recv,
    sface_send, sface_recv, srim_send, srim_recv,
    piece_send, piece_recv, done_send, done_recv, own_sem,
):
    depth = lax.axis_index("depth")
    img = lax.axis_index("img")
    depth_n = lax.axis_size("depth")
    img_n = lax.axis_size("img")
    cells = vel.shape[1]
    cols = vel.shape[2]
    per = cols // CHUNKS
    mine = per // depth_n
    tiles = per // SUB
    layers = cells * depth_n

    def local(c, h):
        if c == 2:
            dst = uz.at[:, h, pl.ds(SUB, cols), :]
        else:
            dst = uxy.at[c, pl.ds(1, cells), h, pl.ds(SUB, cols), :]
        return pltpu.make_async_copy(
            vel.at[c, :, :, pl.ds(h * LANES, LANES)], dst, loc_sem.at[c, h]
        )

    for c in (0, 2, 1):
        for h in range(2):
            local(c, h).start()

    barrier = pltpu.get_barrier_semaphore()

    def greet(j, carry):
        peer = lax.rem(depth + j, depth_n)
        pl.semaphore_signal(barrier, inc=1, device_id={"depth": peer, "img": img})
        return carry

    lax.fori_loop(1, depth_n, greet, 0)

    for step in (1, img_n - 1):
        beside = lax.rem(img + step, img_n)
        pl.semaphore_signal(barrier, inc=1, device_id={"depth": depth, "img": beside})

    zero_tile = jnp.zeros((SUB, LANES), F32)
    for z in range(cells):
        for h in range(2):
            for at in (0, cols + SUB):
                uxy[1, z + 1, h, pl.ds(at, SUB), :] = zero_tile
                uz[z, h, pl.ds(at, SUB), :] = zero_tile
                st[z + 1, h, pl.ds(at, SUB), :] = zero_tile

    pl.semaphore_wait(barrier, depth_n + 1)

    def to_depth(peer):
        return {"depth": peer, "img": img}

    def to_img(peer):
        return {"depth": depth, "img": peer}

    def face(way, k, h):
        layer, slot, peer = ((cells - 1, 0, depth + 1), (0, cells + 1, depth - 1))[way]
        return pltpu.make_async_remote_copy(
            src_ref=vel.at[pl.ds(0, 2), layer, pl.ds(k * per, per), pl.ds(h * LANES, LANES)],
            dst_ref=uxy.at[pl.ds(0, 2), slot, h, pl.ds(SUB + k * per, per), :],
            send_sem=face_send.at[way, k, h],
            recv_sem=face_recv.at[way, k, h],
            device_id=to_depth(peer),
        )

    def strength_face(way, k):
        layer, slot, peer = ((cells, 0, depth + 1), (1, cells + 1, depth - 1))[way]
        rows = pl.ds(SUB + k * per, per)
        return pltpu.make_async_remote_copy(
            src_ref=st.at[layer, :, rows, :],
            dst_ref=st.at[slot, :, rows, :],
            send_sem=sface_send.at[way, k],
            recv_sem=sface_recv.at[way, k],
            device_id=to_depth(peer),
        )

    def rim(way):
        src, dst, peer = ((pack_r, rim_l, img + 1), (pack_l, rim_r, img - 1))[way]
        return pltpu.make_async_remote_copy(
            src_ref=src, dst_ref=dst,
            send_sem=rim_send.at[way], recv_sem=rim_recv.at[way],
            device_id=to_img(peer),
        )

    def strength_rim(way, k):
        src, dst, peer = ((spack_r, srim_l, img + 1), (spack_l, srim_r, img - 1))[way]
        rows = pl.ds(k * per, per)
        return pltpu.make_async_remote_copy(
            src_ref=src.at[rows, :], dst_ref=dst.at[rows, :],
            send_sem=srim_send.at[way, k], recv_sem=srim_recv.at[way, k],
            device_id=to_img(peer),
        )

    has_depth = (depth < depth_n - 1, depth > 0)
    from_depth = (depth > 0, depth < depth_n - 1)
    has_img = (img < img_n - 1, img > 0)
    from_img = (img > 0, img < img_n - 1)

    for k in range(CHUNKS):
        for way in range(2):
            @pl.when(has_depth[way])
            def _(way=way, k=k):
                for h in range(2):
                    face(way, k, h).start()

    lane = lax.broadcasted_iota(jnp.int32, (SUB, LANES), 1)
    first = lane == 0
    last = lane == LANES - 1

    def collect(tile, fields, dst_l, dst_r):
        low = zero_tile
        high = zero_tile
        for at, (v0, v1) in enumerate(fields):
            low = jnp.where(lane == at, v0 if at == 0 else pltpu.roll(v0, at, 1), low)
            high = jnp.where(lane == at, pltpu.roll(v1, at + 1, 1), high)
        rows = pl.ds(pl.multiple_of(tile * SUB, SUB), SUB)
        dst_l[rows, :] = low
        dst_r[rows, :] = high

    for h in range(2):
        local(0, h).wait()
        local(2, h).wait()

    def pack_flow(tile, carry):
        rows = pl.ds(pl.multiple_of(tile * SUB + SUB, SUB), SUB)
        fields = [(uxy[0, z + 1, 0, rows, :], uxy[0, z + 1, 1, rows, :]) for z in range(cells)]
        fields += [(uz[z, 0, rows, :], uz[z, 1, rows, :]) for z in range(cells)]
        collect(tile, fields, pack_l, pack_r)
        return carry

    lax.fori_loop(0, cols // SUB, pack_flow, 0)
    for way in range(2):
        @pl.when(has_img[way])
        def _(way=way):
            rim(way).start()

    for h in range(2):
        local(1, h).wait()
    for way, dst in ((0, rim_l), (1, rim_r)):
        @pl.when(from_img[way])
        def _(way=way):
            rim(way).wait_recv()

        @pl.when(jnp.logical_not(from_img[way]))
        def _(dst=dst):
            dst[...] = jnp.zeros(dst.shape, F32)

    def along_row(v0, v1, left, right):
        p0, p1 = pltpu.roll(v0, LANES - 1, 1), pltpu.roll(v1, LANES - 1, 1)
        m0, m1 = pltpu.roll(v0, 1, 1), pltpu.roll(v1, 1, 1)
        d0 = jnp.where(last, p1, p0) - jnp.where(first, left, m0)
        d1 = jnp.where(last, right, p1) - jnp.where(first, m0, m1)
        return d0, d1

    def edges(tile_l, tile_r, at):
        left = tile_l if at == 0 else pltpu.roll(tile_l, LANES - at, 1)
        right = pltpu.roll(tile_r, LANES - 1 - at, 1)
        return left, right

    def strength_tile(tile, zs):
        base = pl.multiple_of(tile * SUB, SUB)
        rows = pl.ds(pl.multiple_of(base + SUB, SUB), SUB)
        ahead = pl.ds(base + SUB + 1, SUB)
        behind = pl.ds(base + SUB - 1, SUB)
        tile_l, tile_r = rim_l[pl.ds(base, SUB), :], rim_r[pl.ds(base, SUB), :]
        for z in zs:
            dy_ux = along_row(
                uxy[0, z + 1, 0, rows, :], uxy[0, z + 1, 1, rows, :], *edges(tile_l, tile_r, z)
            )
            dy_uz = along_row(
                uz[z, 0, rows, :], uz[z, 1, rows, :], *edges(tile_l, tile_r, cells + z)
            )
            for h in range(2):
                dz_uy = uxy[1, z + 2, h, rows, :] - uxy[1, z, h, rows, :]
                dz_ux = uxy[0, z + 2, h, rows, :] - uxy[0, z, h, rows, :]
                dx_uz = uz[z, h, ahead, :] - uz[z, h, behind, :]
                dx_uy = uxy[1, z + 1, h, ahead, :] - uxy[1, z + 1, h, behind, :]
                cx = dy_uz[h] - dz_uy
                cy = dz_ux - dx_uz
                cz = dx_uy - dy_ux[h]
                square = cx * cx + cy * cy + cz * cz
                st[z + 1, h, rows, :] = square * (0.5 * lax.rsqrt(jnp.maximum(square, TINY)))

    def inner(tile, carry):
        strength_tile(tile, range(1, cells - 1))
        return carry

    lax.fori_loop(0, cols // SUB, inner, 0)

    def outer(tile, carry):
        strength_tile(tile, (0, cells - 1))
        rows = pl.ds(pl.multiple_of(tile * SUB + SUB, SUB), SUB)
        fields = [(st[z + 1, 0, rows, :], st[z + 1, 1, rows, :]) for z in range(cells)]
        collect(tile, fields, spack_l, spack_r)
        return carry

    for k in range(CHUNKS):
        for way, slot in ((0, 0), (1, cells + 1)):
            @pl.when(from_depth[way])
            def _(way=way, k=k):
                for h in range(2):
                    face(way, k, h).wait_recv()

            @pl.when(jnp.logical_not(from_depth[way]))
            def _(slot=slot, k=k):
                for h in range(2):
                    rows = pl.ds(SUB + k * per, per)
                    for c in range(2):
                        uxy[c, slot, h, rows, :] = jnp.zeros((per, LANES), F32)
                    st[slot, h, rows, :] = jnp.zeros((per, LANES), F32)

        lax.fori_loop(k * tiles, (k + 1) * tiles, outer, 0)
        for way in range(2):
            @pl.when(has_depth[way])
            def _(way=way, k=k):
                strength_face(way, k).start()

            @pl.when(has_img[way])
            def _(way=way, k=k):
                strength_rim(way, k).start()

    knots = ext.shape[0]

    def hinges(read):
        steps = [read(k + 1) - read(k) for k in range(knots - 1)]
        return [read(0), steps[0]] + [steps[k] - steps[k - 1] for k in range(1, knots - 1)]

    dense = [g * (1.0 / layers) for g in hinges(lambda k: ext[k])]
    tints = [hinges(lambda k, c=c: emi[c, k]) for c in range(3)]

    def shade(tile, carry):
        base = pl.multiple_of(tile * SUB, SUB)
        here = pl.ds(base, SUB)
        rows = pl.ds(pl.multiple_of(base + SUB, SUB), SUB)
        ahead = pl.ds(base + SUB + 1, SUB)
        behind = pl.ds(base + SUB - 1, SUB)
        tile_l, tile_r = srim_l[here, :], srim_r[here, :]
        clear = [jnp.ones((SUB, LANES), F32)] * 2
        sums = [[None] * knots for _ in range(2)]
        for z in range(cells):
            mid = [st[z + 1, h, rows, :] for h in range(2)]
            dy = along_row(mid[0], mid[1], *edges(tile_l, tile_r, z))
            for h in range(2):
                dx = st[z + 1, h, ahead, :] - st[z + 1, h, behind, :]
                dz = st[z + 2, h, rows, :] - st[z, h, rows, :]
                square = dx * dx + dy[h] * dy[h] + dz * dz
                lean = jnp.abs(0.48 * dx + 0.6 * dy[h] + 0.64 * dz)
                shading = 0.3 + 0.7 * lean * lax.rsqrt(jnp.maximum(square, 4.0))
                level = jnp.minimum(mid[h], 4.0) * ((knots - 1) / 4.0)
                bends = [level] + [jnp.maximum(level - k, 0.0) for k in range(1, knots - 1)]
                optical = dense[0] + dense[1] * level
                for k in range(1, knots - 1):
                    optical = optical + dense[k + 1] * bends[k]
                loss = optical * (
                    1.0 - optical * (0.5 - optical * (1.0 / 6.0 - optical * (1.0 / 24.0)))
                )
                taken = clear[h] * loss
                clear[h] = clear[h] - taken
                lit = taken * shading
                terms = [lit] + [lit * b for b in bends]
                for n in range(knots):
                    sums[h][n] = terms[n] if z == 0 else sums[h][n] + terms[n]
        for h in range(2):
            at = pl.ds(h * LANES, LANES)
            for c in range(3):
                colour = tints[c][0] * sums[h][0]
                for n in range(1, knots):
                    colour = colour + tints[c][n] * sums[h][n]
                part[c, here, at] = colour
            part[3, here, at] = clear[h]
        return carry

    def owned(k, who):
        return pl.ds(pl.multiple_of(k * per + who * mine, SUB), mine)

    def piece(k, to, slot):
        return pltpu.make_async_remote_copy(
            src_ref=part.at[:, owned(k, to), :],
            dst_ref=parts.at[k, slot],
            send_sem=piece_send.at[k, to],
            recv_sem=piece_recv.at[k, slot],
            device_id=to_depth(to),
        )

    def finished(k, to, who):
        return pltpu.make_async_remote_copy(
            src_ref=done.at[k],
            dst_ref=out.at[:, owned(k, who), :],
            send_sem=done_send.at[k, to],
            recv_sem=done_recv.at[k, who],
            device_id=to_depth(to),
        )

    def each_peer(act):
        def step(j, carry):
            act(lax.rem(depth + j, depth_n))
            return carry

        lax.fori_loop(1, depth_n, step, 0)

    for k in range(CHUNKS):
        for way, dst in ((0, srim_l), (1, srim_r)):
            @pl.when(from_depth[way])
            def _(way=way, k=k):
                strength_face(way, k).wait_recv()

            @pl.when(from_img[way])
            def _(way=way, k=k):
                strength_rim(way, k).wait_recv()

            @pl.when(jnp.logical_not(from_img[way]))
            def _(dst=dst, k=k):
                dst[pl.ds(k * per, per), :] = jnp.zeros((per, LANES), F32)

        lax.fori_loop(k * tiles, (k + 1) * tiles, shade, 0)
        each_peer(lambda peer, k=k: piece(k, peer, depth).start())
        parts[k, depth] = part[:, owned(k, depth), :]

    def own(k):
        return pltpu.make_async_copy(done.at[k], out.at[:, owned(k, depth), :], own_sem.at[k])

    for k in range(CHUNKS):
        each_peer(lambda peer, k=k: piece(k, depth, peer).wait_recv())

        def over(s, carry, k=k):
            red, green, blue, clear = carry
            red = red + clear * parts[k, s, 0]
            green = green + clear * parts[k, s, 1]
            blue = blue + clear * parts[k, s, 2]
            return red, green, blue, clear * parts[k, s, 3]

        none = jnp.zeros((mine, part.shape[2]), F32)
        red, green, blue, clear = lax.fori_loop(
            0, depth_n, over, (none, none, none, none + 1.0)
        )
        done[k, 0] = red
        done[k, 1] = green
        done[k, 2] = blue
        done[k, 3] = 1.0 - clear
        each_peer(lambda peer, k=k: finished(k, peer, depth).start())
        own(k).start()

    for k in range(CHUNKS):
        each_peer(lambda peer, k=k: finished(k, depth, peer).wait_recv())
        own(k).wait()

    for k in range(CHUNKS):
        for way in range(2):
            @pl.when(has_depth[way])
            def _(way=way, k=k):
                for h in range(2):
                    face(way, k, h).wait_send()
                strength_face(way, k).wait_send()

            @pl.when(has_img[way])
            def _(way=way, k=k):
                if k == 0:
                    rim(way).wait_send()
                strength_rim(way, k).wait_send()

        def sent(peer, k=k):
            piece(k, peer, depth).wait_send()
            finished(k, peer, depth).wait_send()

        each_peer(sent)


def shards(velocity, emission, extinction):
    flow = velocity[:, :, 0]
    _, cells, cols, rows = flow.shape
    depth_n = lax.axis_size("depth")
    per = cols // CHUNKS
    mine = per // depth_n
    tall = cols + 2 * SUB
    dma = pltpu.SemaphoreType.DMA
    picture = pl.pallas_call(
        kernel,
        out_shape=jax.ShapeDtypeStruct((4, cols, rows), F32),
        in_specs=[
            pl.BlockSpec(memory_space=pl.ANY),
            pl.BlockSpec(memory_space=pltpu.SMEM),
            pl.BlockSpec(memory_space=pltpu.SMEM),
        ],
        out_specs=pl.BlockSpec(memory_space=pl.ANY),
        scratch_shapes=[
            pltpu.VMEM((2, cells + 2, 2, tall, LANES), F32),
            pltpu.VMEM((cells, 2, tall, LANES), F32),
            pltpu.VMEM((cells + 2, 2, tall, LANES), F32),
        ]
        + [pltpu.VMEM((cols, LANES), F32) for _ in range(8)]
        + [
            pltpu.VMEM((4, cols, rows), F32),
            pltpu.VMEM((CHUNKS, depth_n, 4, mine, rows), F32),
            pltpu.VMEM((CHUNKS, 4, mine, rows), F32),
            dma((3, 2)),
            dma((2, CHUNKS, 2)),
            dma((2, CHUNKS, 2)),
            dma((2,)),
            dma((2,)),
            dma((2, CHUNKS)),
            dma((2, CHUNKS)),
            dma((2, CHUNKS)),
            dma((2, CHUNKS)),
            dma((CHUNKS, depth_n)),
            dma((CHUNKS, depth_n)),
            dma((CHUNKS, depth_n)),
            dma((CHUNKS, depth_n)),
            dma((CHUNKS,)),
        ],
        compiler_params=pltpu.CompilerParams(
            collective_id=0, has_side_effects=True, vmem_limit_bytes=48 * 1024 * 1024
        ),
        cost_estimate=pl.CostEstimate(
            flops=100 * cells * cols * rows, bytes_accessed=8 * 1024 * 1024, transcendentals=0
        ),
        name="render",
    )(flow, emission, extinction)
    return picture[:, None]


def solution(mesh):
    return jax.shard_map(
        shards,
        mesh=mesh,
        in_specs=(P(None, "depth", "img", None, None), P(), P()),
        out_specs=P(None, "img", None, None),
        check_vma=False,
    )
```

profile of v0, /device:TPU:184, one launch (start us, length us, event | category | flops | bytes accessed | tf_op | source)
XLA Modules:
  0.0 63.8 jit_solution(13751683490503747338)
XLA Ops:
  0.0 0.0 copy-start
  0.0 0.7 %copy-done = f32[3,8]{1,0:T(4,128)S(1)} copy-done((f32[3,8]{1,0:T(4,128)S(1)}, f32[3,8]{1,0:T(4,128)}, u32[]{:S(2)}) %copy-start) | copy-done | bytes 120
  0.7 0.0 copy-start.1
  0.7 0.7 %copy-done.1 = f32[8]{0:T(128)S(1)} copy-done((f32[8]{0:T(128)S(1)}, f32[8]{0:T(128)}, u32[]{:S(2)}) %copy-start.1) | copy-done | bytes 56
  1.3 61.5 %render.1 = f32[4,256,256]{2,1,0:T(8,128)S(1)} custom-call(f32[3,8,256,256]{3,2,1,0:T(8,128)} %bitcast.5, f32[3,8]{1,0:T(4,128)S(1)} %copy-done, f32[8]{0:T(128)S(1)} %copy-done.1), custom_call_target="tpu_custom_call" | custom-call | flops 52428800 | bytes 8388608 | tf_op jit(solution)/shard_map/render/pallas_call | solution.py:398
  62.9 1.0 %copy.6 = f32[4,1,256,256]{3,2,1,0:T(8,128)} copy(f32[4,1,256,256]{3,2,1,0:T(8,128)S(1)} %bitcast.4) | data formatting | bytes 2097152
Async XLA Ops:
  0.0 0.7 %copy-start = (f32[3,8]{1,0:T(4,128)S(1)}, f32[3,8]{1,0:T(4,128)}, u32[]{:S(2)}) copy-start(f32[3,8]{1,0:T(4,128)} %emi.1) | copy-start | bytes 292
  0.7 0.7 %copy-start.1 = (f32[8]{0:T(128)S(1)}, f32[8]{0:T(128)}, u32[]{:S(2)}) copy-start(f32[8]{0:T(128)} %ext.1) | copy-start | bytes 100
where the time goes:
time: 63.9 us; the launch traced here: 63.8 us
  Pallas kernels  61.5 us (96%)
  local copies, waits for them, and re-layouts  2.31 us (4%)
    pallas_call x1, Pallas kernels, shards(): pl.pallas_call(kernel, out_shape=jax.ShapeDtypeStruct((4, cols, rows), F3...  61.5 us
    unnamed x5, local copies, waits for them, and re-layouts  2.31 us

commit v1 on v0

--- a/solution.py
+++ b/solution.py
@@ -10,17 +10,18 @@
 F32 = jnp.float32
 LANES = 128
 SUB = 8
-CHUNKS = 2
+CHUNKS = 4
+SIDE = 4
 TINY = 1.2e-38
 
 
 def kernel(
-    vel, emi, ext, out,
+    vel, emi_hbm, ext_hbm, out,
     uxy, uz, st, pack_l, pack_r, rim_l, rim_r, spack_l, spack_r, srim_l, srim_r,
-    part, parts, done,
-    loc_sem, face_send, face_recv, rim_send, rim_recv,
+    part, row_parts, row_sum, col_parts, done, emi, ext,
+    table_sem, loc_sem, face_send, face_recv, rim_send, rim_recv,
     sface_send, sface_recv, srim_send, srim_recv,
-    piece_send, piece_recv, done_send, done_recv, own_sem,
+    row_send, row_recv, col_send, col_recv, near_send, near_recv, far_send, far_recv, own_sem,
 ):
     depth = lax.axis_index("depth")
     img = lax.axis_index("img")
@@ -29,7 +30,7 @@
     cells = vel.shape[1]
     cols = vel.shape[2]
     per = cols // CHUNKS
-    mine = per // depth_n
+    gx, gy = depth // SIDE, lax.rem(depth, SIDE)
     tiles = per // SUB
     layers = cells * depth_n
 
@@ -45,6 +46,12 @@
     for c in (0, 2, 1):
         for h in range(2):
             local(c, h).start()
+    tables = [
+        pltpu.make_async_copy(emi_hbm, emi, table_sem.at[0]),
+        pltpu.make_async_copy(ext_hbm, ext, table_sem.at[1]),
+    ]
+    for table in tables:
+        table.start()
 
     barrier = pltpu.get_barrier_semaphore()
 
@@ -96,11 +103,12 @@
             device_id=to_depth(peer),
         )
 
-    def rim(way):
+    def rim(way, k):
         src, dst, peer = ((pack_r, rim_l, img + 1), (pack_l, rim_r, img - 1))[way]
-        return pltpu.make_async_remote_copy(
-            src_ref=src, dst_ref=dst,
-            send_sem=rim_send.at[way], recv_sem=rim_recv.at[way],
+        rows = pl.ds(k * per, per)
+        return pltpu.make_async_remote_copy(
+            src_ref=src.at[rows, :], dst_ref=dst.at[rows, :],
+            send_sem=rim_send.at[way, k], recv_sem=rim_recv.at[way, k],
             device_id=to_img(peer),
         )
 
@@ -150,22 +158,15 @@
         collect(tile, fields, pack_l, pack_r)
         return carry
 
-    lax.fori_loop(0, cols // SUB, pack_flow, 0)
-    for way in range(2):
-        @pl.when(has_img[way])
-        def _(way=way):
-            rim(way).start()
+    for k in range(CHUNKS):
+        lax.fori_loop(k * tiles, (k + 1) * tiles, pack_flow, 0, unroll=4)
+        for way in range(2):
+            @pl.when(has_img[way])
+            def _(way=way, k=k):
+                rim(way, k).start()
 
     for h in range(2):
         local(1, h).wait()
-    for way, dst in ((0, rim_l), (1, rim_r)):
-        @pl.when(from_img[way])
-        def _(way=way):
-            rim(way).wait_recv()
-
-        @pl.when(jnp.logical_not(from_img[way]))
-        def _(dst=dst):
-            dst[...] = jnp.zeros(dst.shape, F32)
 
     def along_row(v0, v1, left, right):
         p0, p1 = pltpu.roll(v0, LANES - 1, 1), pltpu.roll(v1, LANES - 1, 1)
@@ -207,8 +208,6 @@
         strength_tile(tile, range(1, cells - 1))
         return carry
 
-    lax.fori_loop(0, cols // SUB, inner, 0)
-
     def outer(tile, carry):
         strength_tile(tile, (0, cells - 1))
         rows = pl.ds(pl.multiple_of(tile * SUB + SUB, SUB), SUB)
@@ -217,6 +216,16 @@
         return carry
 
     for k in range(CHUNKS):
+        for way, dst in ((0, rim_l), (1, rim_r)):
+            @pl.when(from_img[way])
+            def _(way=way, k=k):
+                rim(way, k).wait_recv()
+
+            @pl.when(jnp.logical_not(from_img[way]))
+            def _(dst=dst, k=k):
+                dst[pl.ds(k * per, per), :] = jnp.zeros((per, LANES), F32)
+
+        lax.fori_loop(k * tiles, (k + 1) * tiles, inner, 0, unroll=2)
         for way, slot in ((0, 0), (1, cells + 1)):
             @pl.when(from_depth[way])
             def _(way=way, k=k):
@@ -231,7 +240,7 @@
                         uxy[c, slot, h, rows, :] = jnp.zeros((per, LANES), F32)
                     st[slot, h, rows, :] = jnp.zeros((per, LANES), F32)
 
-        lax.fori_loop(k * tiles, (k + 1) * tiles, outer, 0)
+        lax.fori_loop(k * tiles, (k + 1) * tiles, outer, 0, unroll=2)
         for way in range(2):
             @pl.when(has_depth[way])
             def _(way=way, k=k):
@@ -241,6 +250,8 @@
             def _(way=way, k=k):
                 strength_rim(way, k).start()
 
+    for table in tables:
+        table.wait()
     knots = ext.shape[0]
 
     def hinges(read):
@@ -283,42 +294,112 @@
                 for n in range(knots):
                     sums[h][n] = terms[n] if z == 0 else sums[h][n] + terms[n]
         for h in range(2):
-            at = pl.ds(h * LANES, LANES)
+            at = (tile // tiles, lax.rem(tile, tiles) // 2, pl.ds(pl.multiple_of(lax.rem(tile, 2) * SUB, SUB), SUB), pl.ds(h * LANES, LANES))
             for c in range(3):
                 colour = tints[c][0] * sums[h][0]
                 for n in range(1, knots):
                     colour = colour + tints[c][n] * sums[h][n]
-                part[c, here, at] = colour
-            part[3, here, at] = clear[h]
+                part[(c, *at)] = colour
+            part[(3, *at)] = clear[h]
         return carry
 
-    def owned(k, who):
-        return pl.ds(pl.multiple_of(k * per + who * mine, SUB), mine)
-
-    def piece(k, to, slot):
-        return pltpu.make_async_remote_copy(
-            src_ref=part.at[:, owned(k, to), :],
-            dst_ref=parts.at[k, slot],
-            send_sem=piece_send.at[k, to],
-            recv_sem=piece_recv.at[k, slot],
-            device_id=to_depth(to),
-        )
-
-    def finished(k, to, who):
+    def place(y):
+        return (
+            pl.ds(pl.multiple_of(y // 2 * SUB, SUB), SUB),
+            pl.ds(pl.multiple_of(lax.rem(y, 2) * LANES, LANES), LANES),
+        )
+
+    def along_y(j):
+        return lax.rem(gy + j, SIDE)
+
+    def along_x(j):
+        return lax.rem(gx + j, SIDE)
+
+    def at_xy(x, y):
+        return to_depth(x * SIDE + y)
+
+    def row_piece(k, y, slot):
+        return pltpu.make_async_remote_copy(
+            src_ref=part.at[:, k, :, *place(y)],
+            dst_ref=row_parts.at[k, slot],
+            send_sem=row_send.at[k, y],
+            recv_sem=row_recv.at[k, slot],
+            device_id=at_xy(gx, y),
+        )
+
+    def col_piece(k, x, slot):
+        return pltpu.make_async_remote_copy(
+            src_ref=row_sum.at[k, x],
+            dst_ref=col_parts.at[k, slot],
+            send_sem=col_send.at[k, x],
+            recv_sem=col_recv.at[k, slot],
+            device_id=at_xy(x, gy),
+        )
+
+    def near(k, y, who):
         return pltpu.make_async_remote_copy(
             src_ref=done.at[k],
-            dst_ref=out.at[:, owned(k, who), :],
-            send_sem=done_send.at[k, to],
-            recv_sem=done_recv.at[k, who],
-            device_id=to_depth(to),
-        )
-
-    def each_peer(act):
-        def step(j, carry):
-            act(lax.rem(depth + j, depth_n))
-            return carry
-
-        lax.fori_loop(1, depth_n, step, 0)
+            dst_ref=out.at[:, k, gx, *place(who)],
+            send_sem=near_send.at[k, y],
+            recv_sem=near_recv.at[k, who],
+            device_id=at_xy(gx, y),
+        )
+
+    def far(k, x, who):
+        return pltpu.make_async_remote_copy(
+            src_ref=out.at[:, k, who],
+            dst_ref=out.at[:, k, who],
+            send_sem=far_send.at[k, x],
+            recv_sem=far_recv.at[k, who],
+            device_id=at_xy(x, gy),
+        )
+
+    def own(k):
+        return pltpu.make_async_copy(done.at[k], out.at[:, k, gx, *place(gy)], own_sem.at[k])
+
+    others = range(1, SIDE)
+
+    def begin(k):
+        for j in others:
+            row_piece(k, along_y(j), gy).start()
+        row_parts[k, gy] = part[:, k, :, *place(gy)]
+
+    def over(tiles_of):
+        total = [tiles_of(0, c) for c in range(4)]
+        for n in range(1, SIDE):
+            for c in range(3):
+                total[c] = total[c] + total[3] * tiles_of(n, c)
+            total[3] = total[3] * tiles_of(n, 3)
+        return total
+
+    def merge_rows(k):
+        for j in others:
+            row_piece(k, gy, along_y(j)).wait_recv()
+        for x in range(SIDE):
+            total = over(lambda n, c, x=x: row_parts[k, n, c, x])
+            for c in range(4):
+                row_sum[k, x, c] = total[c]
+        for j in others:
+            col_piece(k, along_x(j), gx).start()
+        col_parts[k, gx] = row_sum[k, gx]
+
+    def merge_cols(k):
+        for j in others:
+            col_piece(k, gx, along_x(j)).wait_recv()
+        total = over(lambda n, c: col_parts[k, n, c])
+        for c in range(3):
+            done[k, c] = total[c]
+        done[k, 3] = 1.0 - total[3]
+        for j in others:
+            near(k, along_y(j), gy).start()
+        own(k).start()
+
+    def spread(k):
+        own(k).wait()
+        for j in others:
+            near(k, gy, along_y(j)).wait_recv()
+        for j in others:
+            far(k, along_x(j), gx).start()
 
     for k in range(CHUNKS):
         for way, dst in ((0, srim_l), (1, srim_r)):
@@ -334,37 +415,21 @@
             def _(dst=dst, k=k):
                 dst[pl.ds(k * per, per), :] = jnp.zeros((per, LANES), F32)
 
-        lax.fori_loop(k * tiles, (k + 1) * tiles, shade, 0)
-        each_peer(lambda peer, k=k: piece(k, peer, depth).start())
-        parts[k, depth] = part[:, owned(k, depth), :]
-
-    def own(k):
-        return pltpu.make_async_copy(done.at[k], out.at[:, owned(k, depth), :], own_sem.at[k])
-
-    for k in range(CHUNKS):
-        each_peer(lambda peer, k=k: piece(k, depth, peer).wait_recv())
-
-        def over(s, carry, k=k):
-            red, green, blue, clear = carry
-            red = red + clear * parts[k, s, 0]
-            green = green + clear * parts[k, s, 1]
-            blue = blue + clear * parts[k, s, 2]
-            return red, green, blue, clear * parts[k, s, 3]
-
-        none = jnp.zeros((mine, part.shape[2]), F32)
-        red, green, blue, clear = lax.fori_loop(
-            0, depth_n, over, (none, none, none, none + 1.0)
-        )
-        done[k, 0] = red
-        done[k, 1] = green
-        done[k, 2] = blue
-        done[k, 3] = 1.0 - clear
-        each_peer(lambda peer, k=k: finished(k, peer, depth).start())
-        own(k).start()
-
-    for k in range(CHUNKS):
-        each_peer(lambda peer, k=k: finished(k, depth, peer).wait_recv())
-        own(k).wait()
+        lax.fori_loop(k * tiles, (k + 1) * tiles, shade, 0, unroll=2)
+        begin(k)
+        if k >= 1:
+            merge_rows(k - 1)
+        if k >= 2:
+            merge_cols(k - 2)
+        if k >= 3:
+            spread(k - 3)
+
+    for k in range(CHUNKS, CHUNKS + 3):
+        if k - 1 < CHUNKS:
+            merge_rows(k - 1)
+        if k - 2 < CHUNKS:
+            merge_cols(k - 2)
+        spread(k - 3)
 
     for k in range(CHUNKS):
         for way in range(2):
@@ -376,32 +441,30 @@
 
             @pl.when(has_img[way])
             def _(way=way, k=k):
-                if k == 0:
-                    rim(way).wait_send()
+                rim(way, k).wait_send()
                 strength_rim(way, k).wait_send()
 
-        def sent(peer, k=k):
-            piece(k, peer, depth).wait_send()
-            finished(k, peer, depth).wait_send()
-
-        each_peer(sent)
+        for j in others:
+            far(k, gx, along_x(j)).wait_recv()
+            row_piece(k, along_y(j), gy).wait_send()
+            col_piece(k, along_x(j), gx).wait_send()
+            near(k, along_y(j), gy).wait_send()
+            far(k, along_x(j), gx).wait_send()
 
 
 def shards(velocity, emission, extinction):
     flow = velocity[:, :, 0]
     _, cells, cols, rows = flow.shape
-    depth_n = lax.axis_size("depth")
-    per = cols // CHUNKS
-    mine = per // depth_n
+    band = cols // CHUNKS // SIDE
     tall = cols + 2 * SUB
     dma = pltpu.SemaphoreType.DMA
     picture = pl.pallas_call(
         kernel,
-        out_shape=jax.ShapeDtypeStruct((4, cols, rows), F32),
+        out_shape=jax.ShapeDtypeStruct((4, CHUNKS, SIDE, band, rows), F32),
         in_specs=[
             pl.BlockSpec(memory_space=pl.ANY),
-            pl.BlockSpec(memory_space=pltpu.SMEM),
-            pl.BlockSpec(memory_space=pltpu.SMEM),
+            pl.BlockSpec(memory_space=pl.ANY),
+            pl.BlockSpec(memory_space=pl.ANY),
         ],
         out_specs=pl.BlockSpec(memory_space=pl.ANY),
         scratch_shapes=[
@@ -411,24 +474,21 @@
         ]
         + [pltpu.VMEM((cols, LANES), F32) for _ in range(8)]
         + [
-            pltpu.VMEM((4, cols, rows), F32),
-            pltpu.VMEM((CHUNKS, depth_n, 4, mine, rows), F32),
-            pltpu.VMEM((CHUNKS, 4, mine, rows), F32),
+            pltpu.VMEM((4, CHUNKS, SIDE, band, rows), F32),
+            pltpu.VMEM((CHUNKS, SIDE, 4, SIDE, SUB, LANES), F32),
+            pltpu.VMEM((CHUNKS, SIDE, 4, SUB, LANES), F32),
+            pltpu.VMEM((CHUNKS, SIDE, 4, SUB, LANES), F32),
+            pltpu.VMEM((CHUNKS, 4, SUB, LANES), F32),
+            pltpu.SMEM(emission.shape, F32),
+            pltpu.SMEM(extinction.shape, F32),
+            dma((2,)),
             dma((3, 2)),
             dma((2, CHUNKS, 2)),
             dma((2, CHUNKS, 2)),
-            dma((2,)),
-            dma((2,)),
-            dma((2, CHUNKS)),
-            dma((2, CHUNKS)),
-            dma((2, CHUNKS)),
-            dma((2, CHUNKS)),
-            dma((CHUNKS, depth_n)),
-            dma((CHUNKS, depth_n)),
-            dma((CHUNKS, depth_n)),
-            dma((CHUNKS, depth_n)),
-            dma((CHUNKS,)),
-        ],
+        ]
+        + [dma((2, CHUNKS)) for _ in range(6)]
+        + [dma((CHUNKS, SIDE)) for _ in range(8)]
+        + [dma((CHUNKS,))],
         compiler_params=pltpu.CompilerParams(
             collective_id=0, has_side_effects=True, vmem_limit_bytes=48 * 1024 * 1024
         ),
@@ -437,7 +497,7 @@
         ),
         name="render",
     )(flow, emission, extinction)
-    return picture[:, None]
+    return picture.reshape(4, 1, cols, rows)
 
 
 def solution(mesh):

time: 63.9 us -> 56.9 us (0.89)
  the two profiles are of different devices: /device:TPU:184 before, /device:TPU:96 now
where the time goes in v1:
time: 56.9 us; the launch traced here: 55.9 us
  Pallas kernels  53.5 us (94%)
  local copies, waits for them, and re-layouts  2.31 us (4%)
    pallas_call x1, Pallas kernels, shards(): pl.pallas_call(kernel, out_shape=jax.ShapeDtypeStruct((4, CHUNKS, SIDE, b...  53.5 us
    unnamed x5, local copies, waits for them, and re-layouts  2.31 us

profile of v1, /device:TPU:96, one launch (start us, length us, event | category | flops | bytes accessed | tf_op | source)
XLA Modules:
  0.0 55.9 jit_solution(7058284114059939641)
XLA Ops:
  0.0 0.0 copy-start
  0.0 0.7 %copy-done = f32[3,8]{1,0:T(4,128)S(1)} copy-done((f32[3,8]{1,0:T(4,128)S(1)}, f32[3,8]{1,0:T(4,128)}, u32[]{:S(2)}) %copy-start) | copy-done | bytes 120
  0.7 0.0 copy-start.1
  0.7 0.7 %copy-done.1 = f32[8]{0:T(128)S(1)} copy-done((f32[8]{0:T(128)S(1)}, f32[8]{0:T(128)}, u32[]{:S(2)}) %copy-start.1) | copy-done | bytes 56
  1.3 53.5 %render.1 = f32[4,4,4,16,256]{4,3,2,1,0:T(8,128)S(1)} custom-call(f32[3,8,256,256]{3,2,1,0:T(8,128)} %bitcast.5, f32[3,8]{1,0:T(4,128)S(1)} %copy-done, f32[8]{0:T(128)S(1)} %copy-done.1), custom_call_target="tpu_custom_call" | custom-call | flops 52428800 | bytes 8388608 | tf_op jit(solution)/shard_map/render/pallas_call | solution.py:461
  54.9 1.0 %copy.6 = f32[4,1,256,256]{3,2,1,0:T(8,128)} copy(f32[4,1,256,256]{3,2,1,0:T(8,128)S(1)} %bitcast.4) | data formatting | bytes 2097152
Async XLA Ops:
  0.0 0.7 %copy-start = (f32[3,8]{1,0:T(4,128)S(1)}, f32[3,8]{1,0:T(4,128)}, u32[]{:S(2)}) copy-start(f32[3,8]{1,0:T(4,128)} %emi_hbm.1) | copy-start | bytes 292
  0.7 0.7 %copy-start.1 = (f32[8]{0:T(128)S(1)}, f32[8]{0:T(128)}, u32[]{:S(2)}) copy-start(f32[8]{0:T(128)} %ext_hbm.1) | copy-start | bytes 100

commit v2 on v1

--- a/solution.py
+++ b/solution.py
@@ -11,17 +11,21 @@
 LANES = 128
 SUB = 8
 CHUNKS = 4
+LAST = CHUNKS - 1
+EARLY = 3
+HALVED = 2
 SIDE = 4
 TINY = 1.2e-38
 
 
 def kernel(
-    vel, emi_hbm, ext_hbm, out,
+    vel, table_hbm, out,
     uxy, uz, st, pack_l, pack_r, rim_l, rim_r, spack_l, spack_r, srim_l, srim_r,
-    part, row_parts, row_sum, col_parts, done, emi, ext,
+    part, row_parts, row_sum, col_parts, done, parts, table,
     table_sem, loc_sem, face_send, face_recv, rim_send, rim_recv,
     sface_send, sface_recv, srim_send, srim_recv,
-    row_send, row_recv, col_send, col_recv, near_send, near_recv, far_send, far_recv, own_sem,
+    row_send, row_recv, col_send, col_recv, near_send, near_recv, far_send, far_recv,
+    piece_send, piece_recv, side_send, side_recv, cross_send, cross_recv, own_sem,
 ):
     depth = lax.axis_index("depth")
     img = lax.axis_index("img")
@@ -46,12 +50,8 @@
     for c in (0, 2, 1):
         for h in range(2):
             local(c, h).start()
-    tables = [
-        pltpu.make_async_copy(emi_hbm, emi, table_sem.at[0]),
-        pltpu.make_async_copy(ext_hbm, ext, table_sem.at[1]),
-    ]
-    for table in tables:
-        table.start()
+    tables = pltpu.make_async_copy(table_hbm, table, table_sem)
+    tables.start()
 
     barrier = pltpu.get_barrier_semaphore()
 
@@ -126,12 +126,15 @@
     has_img = (img < img_n - 1, img > 0)
     from_img = (img > 0, img < img_n - 1)
 
-    for k in range(CHUNKS):
+    def send_face(k):
         for way in range(2):
             @pl.when(has_depth[way])
-            def _(way=way, k=k):
+            def _(way=way):
                 for h in range(2):
                     face(way, k, h).start()
+
+    for k in range(EARLY):
+        send_face(k)
 
     lane = lax.broadcasted_iota(jnp.int32, (SUB, LANES), 1)
     first = lane == 0
@@ -215,25 +218,27 @@
         collect(tile, fields, spack_l, spack_r)
         return carry
 
-    for k in range(CHUNKS):
+    def inside(k):
         for way, dst in ((0, rim_l), (1, rim_r)):
             @pl.when(from_img[way])
-            def _(way=way, k=k):
+            def _(way=way):
                 rim(way, k).wait_recv()
 
             @pl.when(jnp.logical_not(from_img[way]))
-            def _(dst=dst, k=k):
+            def _(dst=dst):
                 dst[pl.ds(k * per, per), :] = jnp.zeros((per, LANES), F32)
 
         lax.fori_loop(k * tiles, (k + 1) * tiles, inner, 0, unroll=2)
+
+    def faces(k):
         for way, slot in ((0, 0), (1, cells + 1)):
             @pl.when(from_depth[way])
-            def _(way=way, k=k):
+            def _(way=way):
                 for h in range(2):
                     face(way, k, h).wait_recv()
 
             @pl.when(jnp.logical_not(from_depth[way]))
-            def _(slot=slot, k=k):
+            def _(slot=slot):
                 for h in range(2):
                     rows = pl.ds(SUB + k * per, per)
                     for c in range(2):
@@ -243,23 +248,22 @@
         lax.fori_loop(k * tiles, (k + 1) * tiles, outer, 0, unroll=2)
         for way in range(2):
             @pl.when(has_depth[way])
-            def _(way=way, k=k):
+            def _(way=way):
                 strength_face(way, k).start()
 
             @pl.when(has_img[way])
-            def _(way=way, k=k):
+            def _(way=way):
                 strength_rim(way, k).start()
 
-    for table in tables:
-        table.wait()
-    knots = ext.shape[0]
+    tables.wait()
+    knots = table.shape[1]
 
     def hinges(read):
         steps = [read(k + 1) - read(k) for k in range(knots - 1)]
         return [read(0), steps[0]] + [steps[k] - steps[k - 1] for k in range(1, knots - 1)]
 
-    dense = [g * (1.0 / layers) for g in hinges(lambda k: ext[k])]
-    tints = [hinges(lambda k, c=c: emi[c, k]) for c in range(3)]
+    dense = [g * (1.0 / layers) for g in hinges(lambda k: table[3, k])]
+    tints = [hinges(lambda k, c=c: table[c, k]) for c in range(3)]
 
     def shade(tile, carry):
         base = pl.multiple_of(tile * SUB, SUB)
@@ -337,23 +341,60 @@
         )
 
     def near(k, y, who):
-        return pltpu.make_async_remote_copy(
-            src_ref=done.at[k],
-            dst_ref=out.at[:, k, gx, *place(who)],
+        some = pl.ds(0, 2 if k >= HALVED else 4)
+        return pltpu.make_async_remote_copy(
+            src_ref=done.at[k, some],
+            dst_ref=out.at[some, k, gx, *place(who)],
             send_sem=near_send.at[k, y],
             recv_sem=near_recv.at[k, who],
             device_id=at_xy(gx, y),
         )
 
     def far(k, x, who):
-        return pltpu.make_async_remote_copy(
-            src_ref=out.at[:, k, who],
-            dst_ref=out.at[:, k, who],
+        some = pl.ds(0, 2 if k >= HALVED else 4)
+        return pltpu.make_async_remote_copy(
+            src_ref=out.at[some, k, who],
+            dst_ref=out.at[some, k, who],
             send_sem=far_send.at[k, x],
             recv_sem=far_recv.at[k, who],
             device_id=at_xy(x, gy),
         )
 
+    def piece(to, slot):
+        x, y = to // SIDE, lax.rem(to, SIDE)
+        return pltpu.make_async_remote_copy(
+            src_ref=part.at[:, LAST, x, *place(y)],
+            dst_ref=parts.at[slot],
+            send_sem=piece_send.at[to],
+            recv_sem=piece_recv.at[slot],
+            device_id=to_depth(to),
+        )
+
+    def side(k, x, who):
+        return pltpu.make_async_remote_copy(
+            src_ref=done.at[k, pl.ds(2, 2)],
+            dst_ref=out.at[pl.ds(2, 2), k, who, *place(gy)],
+            send_sem=side_send.at[k, x],
+            recv_sem=side_recv.at[k, who],
+            device_id=at_xy(x, gy),
+        )
+
+    def cross(k, y, who):
+        return pltpu.make_async_remote_copy(
+            src_ref=out.at[pl.ds(2, 2), k, :, *place(who)],
+            dst_ref=out.at[pl.ds(2, 2), k, :, *place(who)],
+            send_sem=cross_send.at[k, y],
+            recv_sem=cross_recv.at[k, who],
+            device_id=at_xy(gx, y),
+        )
+
+    def each_peer(act):
+        def step(j, carry):
+            act(lax.rem(depth + j, depth_n))
+            return carry
+
+        lax.fori_loop(1, depth_n, step, 0)
+
     def own(k):
         return pltpu.make_async_copy(done.at[k], out.at[:, k, gx, *place(gy)], own_sem.at[k])
 
@@ -364,9 +405,9 @@
             row_piece(k, along_y(j), gy).start()
         row_parts[k, gy] = part[:, k, :, *place(gy)]
 
-    def over(tiles_of):
+    def over(tiles_of, count=SIDE):
         total = [tiles_of(0, c) for c in range(4)]
-        for n in range(1, SIDE):
+        for n in range(1, count):
             for c in range(3):
                 total[c] = total[c] + total[3] * tiles_of(n, c)
             total[3] = total[3] * tiles_of(n, 3)
@@ -383,16 +424,28 @@
             col_piece(k, along_x(j), gx).start()
         col_parts[k, gx] = row_sum[k, gx]
 
-    def merge_cols(k):
-        for j in others:
-            col_piece(k, gx, along_x(j)).wait_recv()
-        total = over(lambda n, c: col_parts[k, n, c])
+    def finish(k, total):
         for c in range(3):
             done[k, c] = total[c]
         done[k, 3] = 1.0 - total[3]
         for j in others:
             near(k, along_y(j), gy).start()
+            if k >= HALVED:
+                side(k, along_x(j), gx).start()
         own(k).start()
+
+    def merge_cols(k):
+        for j in others:
+            col_piece(k, gx, along_x(j)).wait_recv()
+        finish(k, over(lambda n, c: col_parts[k, n, c]))
+
+    def begin_last():
+        each_peer(lambda peer: piece(peer, depth).start())
+        parts[depth] = part[:, LAST, gx, *place(gy)]
+
+    def merge_last():
+        each_peer(lambda peer: piece(depth, peer).wait_recv())
+        finish(LAST, over(lambda n, c: parts[n, c], SIDE * SIDE))
 
     def spread(k):
         own(k).wait()
@@ -400,36 +453,56 @@
             near(k, gy, along_y(j)).wait_recv()
         for j in others:
             far(k, along_x(j), gx).start()
-
-    for k in range(CHUNKS):
+        if k >= HALVED:
+            for j in others:
+                side(k, gx, along_x(j)).wait_recv()
+            for j in others:
+                cross(k, along_y(j), gy).start()
+
+    def paint(k):
         for way, dst in ((0, srim_l), (1, srim_r)):
             @pl.when(from_depth[way])
-            def _(way=way, k=k):
+            def _(way=way):
                 strength_face(way, k).wait_recv()
 
             @pl.when(from_img[way])
-            def _(way=way, k=k):
+            def _(way=way):
                 strength_rim(way, k).wait_recv()
 
             @pl.when(jnp.logical_not(from_img[way]))
-            def _(dst=dst, k=k):
+            def _(dst=dst):
                 dst[pl.ds(k * per, per), :] = jnp.zeros((per, LANES), F32)
 
         lax.fori_loop(k * tiles, (k + 1) * tiles, shade, 0, unroll=2)
-        begin(k)
-        if k >= 1:
-            merge_rows(k - 1)
-        if k >= 2:
-            merge_cols(k - 2)
-        if k >= 3:
-            spread(k - 3)
-
-    for k in range(CHUNKS, CHUNKS + 3):
-        if k - 1 < CHUNKS:
-            merge_rows(k - 1)
-        if k - 2 < CHUNKS:
-            merge_cols(k - 2)
-        spread(k - 3)
+
+    inside(0)
+    inside(1)
+    faces(0)
+    send_face(3)
+    inside(2)
+    faces(1)
+    inside(3)
+    faces(2)
+    paint(0)
+    begin(0)
+    faces(3)
+    paint(1)
+    begin(1)
+    paint(2)
+    begin(2)
+    merge_rows(0)
+    paint(3)
+    merge_cols(0)
+    begin_last()
+    merge_rows(1)
+    merge_rows(2)
+    merge_cols(1)
+    spread(0)
+    merge_cols(2)
+    merge_last()
+    spread(1)
+    spread(2)
+    spread(3)
 
     for k in range(CHUNKS):
         for way in range(2):
@@ -446,23 +519,29 @@
 
         for j in others:
             far(k, gx, along_x(j)).wait_recv()
-            row_piece(k, along_y(j), gy).wait_send()
-            col_piece(k, along_x(j), gx).wait_send()
+            if k < LAST:
+                row_piece(k, along_y(j), gy).wait_send()
+                col_piece(k, along_x(j), gx).wait_send()
+            if k >= HALVED:
+                cross(k, gy, along_y(j)).wait_recv()
+                side(k, along_x(j), gx).wait_send()
+                cross(k, along_y(j), gy).wait_send()
             near(k, along_y(j), gy).wait_send()
             far(k, along_x(j), gx).wait_send()
+    each_peer(lambda peer: piece(peer, depth).wait_send())
 
 
 def shards(velocity, emission, extinction):
     flow = velocity[:, :, 0]
     _, cells, cols, rows = flow.shape
     band = cols // CHUNKS // SIDE
+    table = jnp.concatenate([emission, extinction[None]], axis=0)
     tall = cols + 2 * SUB
     dma = pltpu.SemaphoreType.DMA
     picture = pl.pallas_call(
         kernel,
         out_shape=jax.ShapeDtypeStruct((4, CHUNKS, SIDE, band, rows), F32),
         in_specs=[
-            pl.BlockSpec(memory_space=pl.ANY),
             pl.BlockSpec(memory_space=pl.ANY),
             pl.BlockSpec(memory_space=pl.ANY),
         ],
@@ -479,15 +558,17 @@
             pltpu.VMEM((CHUNKS, SIDE, 4, SUB, LANES), F32),
             pltpu.VMEM((CHUNKS, SIDE, 4, SUB, LANES), F32),
             pltpu.VMEM((CHUNKS, 4, SUB, LANES), F32),
-            pltpu.SMEM(emission.shape, F32),
-            pltpu.SMEM(extinction.shape, F32),
-            dma((2,)),
+            pltpu.VMEM((SIDE * SIDE, 4, SUB, LANES), F32),
+            pltpu.SMEM(table.shape, F32),
+            dma,
             dma((3, 2)),
             dma((2, CHUNKS, 2)),
             dma((2, CHUNKS, 2)),
         ]
         + [dma((2, CHUNKS)) for _ in range(6)]
         + [dma((CHUNKS, SIDE)) for _ in range(8)]
+        + [dma((SIDE * SIDE,)) for _ in range(2)]
+        + [dma((CHUNKS, SIDE)) for _ in range(4)]
         + [dma((CHUNKS,))],
         compiler_params=pltpu.CompilerParams(
             collective_id=0, has_side_effects=True, vmem_limit_bytes=48 * 1024 * 1024
@@ -496,7 +577,7 @@
             flops=100 * cells * cols * rows, bytes_accessed=8 * 1024 * 1024, transcendentals=0
         ),
         name="render",
-    )(flow, emission, extinction)
+    )(flow, table)
     return picture.reshape(4, 1, cols, rows)
 
 

time: 56.9 us -> 53.7 us (0.944); the launches traced: 55.9 us -> 53.6 us
  Pallas kernels: 53.5 us -> 51.9 us
  local copies, waits for them, and re-layouts: 2.31 us -> 0.97 us
  other arithmetic: 0 us -> 0.71 us
    pallas_call x1, Pallas kernels: 53.5 us -> 51.9 us  [shards(): pl.pallas_call(kernel, out_shape=jax.ShapeDtypeStruct((4, CHUNKS, SIDE, b...]
    unnamed x5 -> x1, local copies, waits for them, and re-layouts: 2.31 us -> 0.97 us
    concatenate x0 -> x1, other arithmetic: none -> 0.71 us  [shards(): table = jnp.concatenate([emission, extinction[None]], axis=0)]
where the time goes in v2:
time: 53.7 us; the launch traced here: 53.6 us
  Pallas kernels  51.9 us (97%)
  local copies, waits for them, and re-layouts  0.97 us (2%)
  other arithmetic  0.71 us (1%)
    pallas_call x1, Pallas kernels, shards(): pl.pallas_call(kernel, out_shape=jax.ShapeDtypeStruct((4, CHUNKS, SIDE, b...  51.9 us

profile of v2, /device:TPU:96, one launch (start us, length us, event | category | flops | bytes accessed | tf_op | source)
XLA Modules:
  0.0 53.6 jit_solution(18236969550147635164)
XLA Ops:
  0.0 0.7 %pad_maximum_fusion.table_hbm = f32[4,8]{1,0:T(4,128)S(1)} fusion(f32[1,8]{1,0:T(1,128)} %bitcast.7, f32[3,8]{1,0:T(4,128)} %param.4), kind=kLoop, calls=%fused_computation | loop fusion | flops 32 | bytes 256 | tf_op jit(solution)/shard_map/concatenate | solution.py:538
  0.7 51.9 %render.1 = f32[4,4,4,16,256]{4,3,2,1,0:T(8,128)S(1)} custom-call(f32[3,8,256,256]{3,2,1,0:T(8,128)} %bitcast.6, f32[4,8]{1,0:T(4,128)S(1)} %pad_maximum_fusion.table_hbm), custom_call_target="tpu_custom_call" | custom-call | flops 52428800 | bytes 8388608 | tf_op jit(solution)/shard_map/render/pallas_call | solution.py:541
  52.6 1.0 %copy.6 = f32[4,1,256,256]{3,2,1,0:T(8,128)} copy(f32[4,1,256,256]{3,2,1,0:T(8,128)S(1)} %bitcast.5) | data formatting | bytes 2097152

commit v3 on v2

--- a/solution.py
+++ b/solution.py
@@ -13,15 +13,15 @@
 CHUNKS = 4
 LAST = CHUNKS - 1
 EARLY = 3
-HALVED = 2
+Y_FIRST = 2
 SIDE = 4
 TINY = 1.2e-38
 
 
 def kernel(
-    vel, table_hbm, out,
+    vel, emi_hbm, ext_hbm, out,
     uxy, uz, st, pack_l, pack_r, rim_l, rim_r, spack_l, spack_r, srim_l, srim_r,
-    part, row_parts, row_sum, col_parts, done, parts, table,
+    part, row_parts, row_sum, col_parts, done, parts, emi, ext,
     table_sem, loc_sem, face_send, face_recv, rim_send, rim_recv,
     sface_send, sface_recv, srim_send, srim_recv,
     row_send, row_recv, col_send, col_recv, near_send, near_recv, far_send, far_recv,
@@ -38,20 +38,17 @@
     tiles = per // SUB
     layers = cells * depth_n
 
+    def take(sem, like):
+        pltpu.make_async_copy(like, like, sem).wait()
+
     def local(c, h):
         if c == 2:
             dst = uz.at[:, h, pl.ds(SUB, cols), :]
         else:
             dst = uxy.at[c, pl.ds(1, cells), h, pl.ds(SUB, cols), :]
         return pltpu.make_async_copy(
-            vel.at[c, :, :, pl.ds(h * LANES, LANES)], dst, loc_sem.at[c, h]
-        )
-
-    for c in (0, 2, 1):
-        for h in range(2):
-            local(c, h).start()
-    tables = pltpu.make_async_copy(table_hbm, table, table_sem)
-    tables.start()
+            vel.at[c, :, :, pl.ds(h * LANES, LANES)], dst, loc_sem.at[c % 2]
+        )
 
     barrier = pltpu.get_barrier_semaphore()
 
@@ -65,6 +62,16 @@
     for step in (1, img_n - 1):
         beside = lax.rem(img + step, img_n)
         pl.semaphore_signal(barrier, inc=1, device_id={"depth": depth, "img": beside})
+
+    for c in (0, 2, 1):
+        for h in range(2):
+            local(c, h).start()
+    tables = [
+        pltpu.make_async_copy(emi_hbm, emi, table_sem.at[0]),
+        pltpu.make_async_copy(ext_hbm, ext, table_sem.at[1]),
+    ]
+    for table in tables:
+        table.start()
 
     zero_tile = jnp.zeros((SUB, LANES), F32)
     for z in range(cells):
@@ -87,8 +94,8 @@
         return pltpu.make_async_remote_copy(
             src_ref=vel.at[pl.ds(0, 2), layer, pl.ds(k * per, per), pl.ds(h * LANES, LANES)],
             dst_ref=uxy.at[pl.ds(0, 2), slot, h, pl.ds(SUB + k * per, per), :],
-            send_sem=face_send.at[way, k, h],
-            recv_sem=face_recv.at[way, k, h],
+            send_sem=face_send.at[way],
+            recv_sem=face_recv.at[way, k],
             device_id=to_depth(peer),
         )
 
@@ -98,7 +105,7 @@
         return pltpu.make_async_remote_copy(
             src_ref=st.at[layer, :, rows, :],
             dst_ref=st.at[slot, :, rows, :],
-            send_sem=sface_send.at[way, k],
+            send_sem=sface_send.at[way],
             recv_sem=sface_recv.at[way, k],
             device_id=to_depth(peer),
         )
@@ -108,7 +115,7 @@
         rows = pl.ds(k * per, per)
         return pltpu.make_async_remote_copy(
             src_ref=src.at[rows, :], dst_ref=dst.at[rows, :],
-            send_sem=rim_send.at[way, k], recv_sem=rim_recv.at[way, k],
+            send_sem=rim_send.at[way], recv_sem=rim_recv.at[way, k],
             device_id=to_img(peer),
         )
 
@@ -117,7 +124,7 @@
         rows = pl.ds(k * per, per)
         return pltpu.make_async_remote_copy(
             src_ref=src.at[rows, :], dst_ref=dst.at[rows, :],
-            send_sem=srim_send.at[way, k], recv_sem=srim_recv.at[way, k],
+            send_sem=srim_send.at[way], recv_sem=srim_recv.at[way, k],
             device_id=to_img(peer),
         )
 
@@ -150,9 +157,8 @@
         dst_l[rows, :] = low
         dst_r[rows, :] = high
 
-    for h in range(2):
-        local(0, h).wait()
-        local(2, h).wait()
+    inner_rows = pl.ds(SUB, cols)
+    take(loc_sem.at[0], uxy.at[:, pl.ds(1, cells), :, inner_rows, :])
 
     def pack_flow(tile, carry):
         rows = pl.ds(pl.multiple_of(tile * SUB + SUB, SUB), SUB)
@@ -168,8 +174,7 @@
             def _(way=way, k=k):
                 rim(way, k).start()
 
-    for h in range(2):
-        local(1, h).wait()
+    take(loc_sem.at[1], uxy.at[1, pl.ds(1, cells), :, inner_rows, :])
 
     def along_row(v0, v1, left, right):
         p0, p1 = pltpu.roll(v0, LANES - 1, 1), pltpu.roll(v1, LANES - 1, 1)
@@ -234,8 +239,9 @@
         for way, slot in ((0, 0), (1, cells + 1)):
             @pl.when(from_depth[way])
             def _(way=way):
-                for h in range(2):
-                    face(way, k, h).wait_recv()
+                slot = (0, cells + 1)[way]
+                rows = pl.ds(SUB + k * per, per)
+                take(face_recv.at[way, k], uxy.at[:, slot, :, rows, :])
 
             @pl.when(jnp.logical_not(from_depth[way]))
             def _(slot=slot):
@@ -255,15 +261,16 @@
             def _(way=way):
                 strength_rim(way, k).start()
 
-    tables.wait()
-    knots = table.shape[1]
+    for table in tables:
+        table.wait()
+    knots = ext.shape[0]
 
     def hinges(read):
         steps = [read(k + 1) - read(k) for k in range(knots - 1)]
         return [read(0), steps[0]] + [steps[k] - steps[k - 1] for k in range(1, knots - 1)]
 
-    dense = [g * (1.0 / layers) for g in hinges(lambda k: table[3, k])]
-    tints = [hinges(lambda k, c=c: table[c, k]) for c in range(3)]
+    dense = [g * (1.0 / layers) for g in hinges(lambda k: ext[k])]
+    tints = [hinges(lambda k, c=c: emi[c, k]) for c in range(3)]
 
     def shade(tile, carry):
         base = pl.multiple_of(tile * SUB, SUB)
@@ -326,8 +333,8 @@
         return pltpu.make_async_remote_copy(
             src_ref=part.at[:, k, :, *place(y)],
             dst_ref=row_parts.at[k, slot],
-            send_sem=row_send.at[k, y],
-            recv_sem=row_recv.at[k, slot],
+            send_sem=row_send,
+            recv_sem=row_recv.at[k],
             device_id=at_xy(gx, y),
         )
 
@@ -335,56 +342,58 @@
         return pltpu.make_async_remote_copy(
             src_ref=row_sum.at[k, x],
             dst_ref=col_parts.at[k, slot],
-            send_sem=col_send.at[k, x],
-            recv_sem=col_recv.at[k, slot],
+            send_sem=col_send,
+            recv_sem=col_recv.at[k],
             device_id=at_xy(x, gy),
         )
 
     def near(k, y, who):
-        some = pl.ds(0, 2 if k >= HALVED else 4)
+        some = pl.ds(0, Y_FIRST)
         return pltpu.make_async_remote_copy(
             src_ref=done.at[k, some],
             dst_ref=out.at[some, k, gx, *place(who)],
-            send_sem=near_send.at[k, y],
-            recv_sem=near_recv.at[k, who],
+            send_sem=near_send,
+            recv_sem=near_recv.at[k],
             device_id=at_xy(gx, y),
         )
 
     def far(k, x, who):
-        some = pl.ds(0, 2 if k >= HALVED else 4)
+        some = pl.ds(0, Y_FIRST)
         return pltpu.make_async_remote_copy(
             src_ref=out.at[some, k, who],
             dst_ref=out.at[some, k, who],
-            send_sem=far_send.at[k, x],
-            recv_sem=far_recv.at[k, who],
+            send_sem=far_send,
+            recv_sem=far_recv.at[k],
             device_id=at_xy(x, gy),
         )
 
-    def piece(to, slot):
+    def piece(k, to, slot):
         x, y = to // SIDE, lax.rem(to, SIDE)
         return pltpu.make_async_remote_copy(
-            src_ref=part.at[:, LAST, x, *place(y)],
+            src_ref=part.at[:, k, x, *place(y)],
             dst_ref=parts.at[slot],
-            send_sem=piece_send.at[to],
-            recv_sem=piece_recv.at[slot],
+            send_sem=piece_send,
+            recv_sem=piece_recv,
             device_id=to_depth(to),
         )
 
     def side(k, x, who):
-        return pltpu.make_async_remote_copy(
-            src_ref=done.at[k, pl.ds(2, 2)],
-            dst_ref=out.at[pl.ds(2, 2), k, who, *place(gy)],
-            send_sem=side_send.at[k, x],
-            recv_sem=side_recv.at[k, who],
+        some = pl.ds(Y_FIRST, 4 - Y_FIRST)
+        return pltpu.make_async_remote_copy(
+            src_ref=done.at[k, some],
+            dst_ref=out.at[some, k, who, *place(gy)],
+            send_sem=side_send,
+            recv_sem=side_recv.at[k],
             device_id=at_xy(x, gy),
         )
 
     def cross(k, y, who):
-        return pltpu.make_async_remote_copy(
-            src_ref=out.at[pl.ds(2, 2), k, :, *place(who)],
-            dst_ref=out.at[pl.ds(2, 2), k, :, *place(who)],
-            send_sem=cross_send.at[k, y],
-            recv_sem=cross_recv.at[k, who],
+        some = pl.ds(Y_FIRST, 4 - Y_FIRST)
+        return pltpu.make_async_remote_copy(
+            src_ref=out.at[some, k, :, *place(who)],
+            dst_ref=out.at[some, k, :, *place(who)],
+            send_sem=cross_send,
+            recv_sem=cross_recv.at[k],
             device_id=at_xy(gx, y),
         )
 
@@ -399,6 +408,8 @@
         return pltpu.make_async_copy(done.at[k], out.at[:, k, gx, *place(gy)], own_sem.at[k])
 
     others = range(1, SIDE)
+    three = pl.ds(0, SIDE - 1)
+    low, high = pl.ds(0, Y_FIRST), pl.ds(Y_FIRST, 4 - Y_FIRST)
 
     def begin(k):
         for j in others:
@@ -414,8 +425,7 @@
         return total
 
     def merge_rows(k):
-        for j in others:
-            row_piece(k, gy, along_y(j)).wait_recv()
+        take(row_recv.at[k], row_parts.at[k, three])
         for x in range(SIDE):
             total = over(lambda n, c, x=x: row_parts[k, n, c, x])
             for c in range(4):
@@ -430,34 +440,29 @@
         done[k, 3] = 1.0 - total[3]
         for j in others:
             near(k, along_y(j), gy).start()
-            if k >= HALVED:
-                side(k, along_x(j), gx).start()
+            side(k, along_x(j), gx).start()
         own(k).start()
 
     def merge_cols(k):
-        for j in others:
-            col_piece(k, gx, along_x(j)).wait_recv()
+        take(col_recv.at[k], col_parts.at[k, three])
         finish(k, over(lambda n, c: col_parts[k, n, c]))
 
-    def begin_last():
-        each_peer(lambda peer: piece(peer, depth).start())
-        parts[depth] = part[:, LAST, gx, *place(gy)]
-
-    def merge_last():
-        each_peer(lambda peer: piece(depth, peer).wait_recv())
-        finish(LAST, over(lambda n, c: parts[n, c], SIDE * SIDE))
+    def begin_direct(k):
+        each_peer(lambda peer: piece(k, peer, depth).start())
+        parts[depth] = part[:, k, gx, *place(gy)]
+
+    def merge_direct(k):
+        take(piece_recv, parts.at[pl.ds(0, depth_n - 1)])
+        finish(k, over(lambda n, c: parts[n, c], SIDE * SIDE))
 
     def spread(k):
         own(k).wait()
-        for j in others:
-            near(k, gy, along_y(j)).wait_recv()
+        take(near_recv.at[k], col_parts.at[0, three, low])
         for j in others:
             far(k, along_x(j), gx).start()
-        if k >= HALVED:
-            for j in others:
-                side(k, gx, along_x(j)).wait_recv()
-            for j in others:
-                cross(k, along_y(j), gy).start()
+        take(side_recv.at[k], col_parts.at[0, three, high])
+        for j in others:
+            cross(k, along_y(j), gy).start()
 
     def paint(k):
         for way, dst in ((0, srim_l), (1, srim_r)):
@@ -474,6 +479,22 @@
                 dst[pl.ds(k * per, per), :] = jnp.zeros((per, LANES), F32)
 
         lax.fori_loop(k * tiles, (k + 1) * tiles, shade, 0, unroll=2)
+
+    def settle():
+        for way, slot in ((0, 0), (1, cells + 1)):
+            @pl.when(has_depth[way])
+            def _(way=way, slot=slot):
+                take(face_send.at[way], uxy.at[:, slot, :, inner_rows, :])
+                take(sface_send.at[way], st.at[slot, :, inner_rows, :])
+
+            @pl.when(has_img[way])
+            def _(way=way):
+                take(rim_send.at[way], pack_l)
+                take(srim_send.at[way], spack_l)
+
+        take(row_send, row_parts.at[:, three])
+        take(col_send, col_parts.at[:, three])
+        take(piece_send, parts.at[pl.ds(0, depth_n - 1)])
 
     inside(0)
     inside(1)
@@ -492,56 +513,39 @@
     begin(2)
     merge_rows(0)
     paint(3)
+    merge_rows(1)
     merge_cols(0)
-    begin_last()
-    merge_rows(1)
+    begin_direct(3)
     merge_rows(2)
     merge_cols(1)
     spread(0)
     merge_cols(2)
-    merge_last()
+    merge_direct(3)
     spread(1)
+    settle()
     spread(2)
     spread(3)
 
+    take(near_send, col_parts.at[:, :, low])
+    take(side_send, col_parts.at[:, :, high])
     for k in range(CHUNKS):
-        for way in range(2):
-            @pl.when(has_depth[way])
-            def _(way=way, k=k):
-                for h in range(2):
-                    face(way, k, h).wait_send()
-                strength_face(way, k).wait_send()
-
-            @pl.when(has_img[way])
-            def _(way=way, k=k):
-                rim(way, k).wait_send()
-                strength_rim(way, k).wait_send()
-
-        for j in others:
-            far(k, gx, along_x(j)).wait_recv()
-            if k < LAST:
-                row_piece(k, along_y(j), gy).wait_send()
-                col_piece(k, along_x(j), gx).wait_send()
-            if k >= HALVED:
-                cross(k, gy, along_y(j)).wait_recv()
-                side(k, along_x(j), gx).wait_send()
-                cross(k, along_y(j), gy).wait_send()
-            near(k, along_y(j), gy).wait_send()
-            far(k, along_x(j), gx).wait_send()
-    each_peer(lambda peer: piece(peer, depth).wait_send())
+        take(far_recv.at[k], out.at[low, k, three])
+        take(cross_recv.at[k], out.at[high, k, three])
+    take(far_send, out.at[low, :, three])
+    take(cross_send, out.at[high, :, three])
 
 
 def shards(velocity, emission, extinction):
     flow = velocity[:, :, 0]
     _, cells, cols, rows = flow.shape
     band = cols // CHUNKS // SIDE
-    table = jnp.concatenate([emission, extinction[None]], axis=0)
     tall = cols + 2 * SUB
     dma = pltpu.SemaphoreType.DMA
     picture = pl.pallas_call(
         kernel,
         out_shape=jax.ShapeDtypeStruct((4, CHUNKS, SIDE, band, rows), F32),
         in_specs=[
+            pl.BlockSpec(memory_space=pl.ANY),
             pl.BlockSpec(memory_space=pl.ANY),
             pl.BlockSpec(memory_space=pl.ANY),
         ],
@@ -554,21 +558,21 @@
         + [pltpu.VMEM((cols, LANES), F32) for _ in range(8)]
         + [
             pltpu.VMEM((4, CHUNKS, SIDE, band, rows), F32),
-            pltpu.VMEM((CHUNKS, SIDE, 4, SIDE, SUB, LANES), F32),
-            pltpu.VMEM((CHUNKS, SIDE, 4, SUB, LANES), F32),
-            pltpu.VMEM((CHUNKS, SIDE, 4, SUB, LANES), F32),
+            pltpu.VMEM((LAST, SIDE, 4, SIDE, SUB, LANES), F32),
+            pltpu.VMEM((LAST, SIDE, 4, SUB, LANES), F32),
+            pltpu.VMEM((LAST, SIDE, 4, SUB, LANES), F32),
             pltpu.VMEM((CHUNKS, 4, SUB, LANES), F32),
             pltpu.VMEM((SIDE * SIDE, 4, SUB, LANES), F32),
-            pltpu.SMEM(table.shape, F32),
-            dma,
-            dma((3, 2)),
-            dma((2, CHUNKS, 2)),
-            dma((2, CHUNKS, 2)),
+            pltpu.SMEM(emission.shape, F32),
+            pltpu.SMEM(extinction.shape, F32),
+            dma((2,)),
+            dma((2,)),
         ]
-        + [dma((2, CHUNKS)) for _ in range(6)]
-        + [dma((CHUNKS, SIDE)) for _ in range(8)]
-        + [dma((SIDE * SIDE,)) for _ in range(2)]
-        + [dma((CHUNKS, SIDE)) for _ in range(4)]
+        + [dma((2,)), dma((2, CHUNKS))] * 4
+        + [dma, dma((LAST,))] * 2
+        + [dma, dma((CHUNKS,))] * 2
+        + [dma, dma]
+        + [dma, dma((CHUNKS,))] * 2
         + [dma((CHUNKS,))],
         compiler_params=pltpu.CompilerParams(
             collective_id=0, has_side_effects=True, vmem_limit_bytes=48 * 1024 * 1024
@@ -577,7 +581,11 @@
             flops=100 * cells * cols * rows, bytes_accessed=8 * 1024 * 1024, transcendentals=0
         ),
         name="render",
-    )(flow, table)
+    )(
+        flow,
+        pltpu.with_memory_space_constraint(emission, pltpu.HBM),
+        pltpu.with_memory_space_constraint(extinction, pltpu.HBM),
+    )
     return picture.reshape(4, 1, cols, rows)
 
 

time: 53.7 us -> 49.4 us (0.920)
  Pallas kernels: 51.9 us -> 48.4 us
  other arithmetic: 0.71 us -> 0 us
    pallas_call x1, Pallas kernels: 51.9 us -> 48.4 us  [shards(): pl.pallas_call(kernel, out_shape=jax.ShapeDtypeStruct((4, CHUNKS, SIDE, b...]
    concatenate x1 -> x0, other arithmetic: 0.71 us -> none  [shards(): table = jnp.concatenate([emission, extinction[None]], axis=0)]
where the time goes in v3:
time: 49.4 us
  Pallas kernels  48.4 us (98%)
  local copies, waits for them, and re-layouts  0.97 us (2%)
    pallas_call x1, Pallas kernels, shards(): pl.pallas_call(kernel, out_shape=jax.ShapeDtypeStruct((4, CHUNKS, SIDE, b...  48.4 us

profile of v3, /device:TPU:96, one launch (start us, length us, event | category | flops | bytes accessed | tf_op | source)
XLA Modules:
  0.0 49.4 jit_solution(16946243929195994924)
XLA Ops:
  0.0 48.4 %render.1 = f32[4,4,4,16,256]{4,3,2,1,0:T(8,128)S(1)} custom-call(f32[3,8,256,256]{3,2,1,0:T(8,128)} %bitcast.5, f32[3,8]{1,0:T(4,128)} %emi_hbm.1, f32[8]{0:T(128)} %ext_hbm.1), custom_call_target="tpu_custom_call" | custom-call | flops 52428800 | bytes 8388608 | tf_op jit(solution)/shard_map/render/pallas_call | solution.py:544
  48.4 1.0 %copy.6 = f32[4,1,256,256]{3,2,1,0:T(8,128)} copy(f32[4,1,256,256]{3,2,1,0:T(8,128)S(1)} %bitcast.4) | data formatting | bytes 2097152

commit v4 on v3

--- a/solution.py
+++ b/solution.py
@@ -23,9 +23,9 @@
     uxy, uz, st, pack_l, pack_r, rim_l, rim_r, spack_l, spack_r, srim_l, srim_r,
     part, row_parts, row_sum, col_parts, done, parts, emi, ext,
     table_sem, loc_sem, face_send, face_recv, rim_send, rim_recv,
-    sface_send, sface_recv, srim_send, srim_recv,
+    sface_recv, srim_recv,
     row_send, row_recv, col_send, col_recv, near_send, near_recv, far_send, far_recv,
-    piece_send, piece_recv, side_send, side_recv, cross_send, cross_recv, own_sem,
+    piece_send, piece_recv, side_recv, own_sem,
 ):
     depth = lax.axis_index("depth")
     img = lax.axis_index("img")
@@ -105,7 +105,7 @@
         return pltpu.make_async_remote_copy(
             src_ref=st.at[layer, :, rows, :],
             dst_ref=st.at[slot, :, rows, :],
-            send_sem=sface_send.at[way],
+            send_sem=face_send.at[way],
             recv_sem=sface_recv.at[way, k],
             device_id=to_depth(peer),
         )
@@ -124,7 +124,7 @@
         rows = pl.ds(k * per, per)
         return pltpu.make_async_remote_copy(
             src_ref=src.at[rows, :], dst_ref=dst.at[rows, :],
-            send_sem=srim_send.at[way], recv_sem=srim_recv.at[way, k],
+            send_sem=rim_send.at[way], recv_sem=srim_recv.at[way, k],
             device_id=to_img(peer),
         )
 
@@ -363,7 +363,7 @@
             src_ref=out.at[some, k, who],
             dst_ref=out.at[some, k, who],
             send_sem=far_send,
-            recv_sem=far_recv.at[k],
+            recv_sem=far_recv,
             device_id=at_xy(x, gy),
         )
 
@@ -382,7 +382,7 @@
         return pltpu.make_async_remote_copy(
             src_ref=done.at[k, some],
             dst_ref=out.at[some, k, who, *place(gy)],
-            send_sem=side_send,
+            send_sem=near_send,
             recv_sem=side_recv.at[k],
             device_id=at_xy(x, gy),
         )
@@ -392,8 +392,8 @@
         return pltpu.make_async_remote_copy(
             src_ref=out.at[some, k, :, *place(who)],
             dst_ref=out.at[some, k, :, *place(who)],
-            send_sem=cross_send,
-            recv_sem=cross_recv.at[k],
+            send_sem=far_send,
+            recv_sem=far_recv,
             device_id=at_xy(gx, y),
         )
 
@@ -484,13 +484,11 @@
         for way, slot in ((0, 0), (1, cells + 1)):
             @pl.when(has_depth[way])
             def _(way=way, slot=slot):
-                take(face_send.at[way], uxy.at[:, slot, :, inner_rows, :])
-                take(sface_send.at[way], st.at[slot, :, inner_rows, :])
+                take(face_send.at[way], uxy.at[0, pl.ds(0, 3), :, inner_rows, :])
 
             @pl.when(has_img[way])
-            def _(way=way):
-                take(rim_send.at[way], pack_l)
-                take(srim_send.at[way], spack_l)
+            def _(way=way, slot=slot):
+                take(rim_send.at[way], st.at[slot, :, inner_rows, :])
 
         take(row_send, row_parts.at[:, three])
         take(col_send, col_parts.at[:, three])
@@ -526,13 +524,9 @@
     spread(2)
     spread(3)
 
-    take(near_send, col_parts.at[:, :, low])
-    take(side_send, col_parts.at[:, :, high])
-    for k in range(CHUNKS):
-        take(far_recv.at[k], out.at[low, k, three])
-        take(cross_recv.at[k], out.at[high, k, three])
-    take(far_send, out.at[low, :, three])
-    take(cross_send, out.at[high, :, three])
+    take(near_send, col_parts)
+    take(far_recv, out.at[:, :, three])
+    take(far_send, out.at[:, :, three])
 
 
 def shards(velocity, emission, extinction):
@@ -568,12 +562,12 @@
             dma((2,)),
             dma((2,)),
         ]
-        + [dma((2,)), dma((2, CHUNKS))] * 4
+        + [dma((2,)), dma((2, CHUNKS))] * 2
+        + [dma((2, CHUNKS))] * 2
         + [dma, dma((LAST,))] * 2
-        + [dma, dma((CHUNKS,))] * 2
-        + [dma, dma]
-        + [dma, dma((CHUNKS,))] * 2
-        + [dma((CHUNKS,))],
+        + [dma, dma((CHUNKS,))]
+        + [dma] * 4
+        + [dma((CHUNKS,))] * 2,
         compiler_params=pltpu.CompilerParams(
             collective_id=0, has_side_effects=True, vmem_limit_bytes=48 * 1024 * 1024
         ),

time: 49.4 us -> 49.3 us (level)
  no operation moved by 1% of the time
where the time goes in v4:
time: 49.3 us; the launch traced here: 49.2 us
  Pallas kernels  48.3 us (98%)
  local copies, waits for them, and re-layouts  0.97 us (2%)
    pallas_call x1, Pallas kernels, shards(): pl.pallas_call(kernel, out_shape=jax.ShapeDtypeStruct((4, CHUNKS, SIDE, b...  48.3 us

profile of v4, /device:TPU:96, one launch (start us, length us, event | category | flops | bytes accessed | tf_op | source)
XLA Modules:
  0.0 49.2 jit_solution(8906565246308379318)
XLA Ops:
  0.0 48.3 %render.1 = f32[4,4,4,16,256]{4,3,2,1,0:T(8,128)S(1)} custom-call(f32[3,8,256,256]{3,2,1,0:T(8,128)} %bitcast.5, f32[3,8]{1,0:T(4,128)} %emi_hbm.1, f32[8]{0:T(128)} %ext_hbm.1), custom_call_target="tpu_custom_call" | custom-call | flops 52428800 | bytes 8388608 | tf_op jit(solution)/shard_map/render/pallas_call | solution.py:538
  48.3 1.0 %copy.6 = f32[4,1,256,256]{3,2,1,0:T(8,128)} copy(f32[4,1,256,256]{3,2,1,0:T(8,128)S(1)} %bitcast.4) | data formatting | bytes 2097152
